TPU v7x, 32 devices: a whole 2x2x4 slice. The times are simulated.
32 devices in a mesh: inner: 16 (over z, y, x), outer: 2 (over core).
Axes of the slice: x: 2, y: 2, z: 4, core: 2. Of those that a mesh axis runs over, the one named last changes fastest.
Arguments:
- feats_first: bfloat16 [2, 4096, 2048], P('outer', 'inner'), may hold values from -4 to 8
- feats_second: bfloat16 [2, 4096, 2048], P('outer', 'inner'), may hold values from -4 to 8
- expander: bfloat16 [2048, 1024], P('inner'), may hold values from -0.125 to 0.125
- tile_count: int32 [2, 16], replicated, may hold values from 64 to 256, as said below
- match_dev: int32 [2, 4096, 1], P('outer', 'inner'), may hold values from 0 to 15; in each aligned block of 256 rows (0 to 255, 256 to 511, ..., all dimensions but the last counted through in order) at most 48 rows name the same one
- match_tile: int32 [2, 4096], P('outer', 'inner'), may hold values from 0 to 255
Outputs:
- covariance: float32 [1024, 1024], P('inner')
- invariance: float32 [2, 4096], P('outer', 'inner')
Inputs may be any that keep to these rules, and one draw needn't show every extreme that they name: `tile_count`: for every slide some device has all 256 tiles live; the others at least a quarter. `match_dev`: at most 48 tiles of one device name the same device.
All inputs are finite; a program needn't handle non-finite values.
Results may differ from a plain program's by a relative error of at most 0.00135.
Values may be sent and summed in bfloat16 or wider, within the bound.
A program may use at most 64 MiB of HBM per device.

v0:
```python
import jax
import jax.numpy as jnp
from jax import lax
from jax.sharding import PartitionSpec as P


def shards(feats_first, feats_second, expander, tile_count, match_dev, match_tile):
    first_rows = feats_first[0]
    second_rows = feats_second[0]
    tile_rows = first_rows.shape[0]
    expand_width = expander.shape[1]
    group_size = lax.axis_size("inner")
    capacity = -(-max(2, 3 * tile_rows // group_size) // 16) * 16
    slots = group_size * capacity
    inner_pos = lax.axis_index("inner")
    outer_pos = lax.axis_index("outer")
    target_dev = match_dev[0, :, 0]
    target_tile = match_tile[0]
    row_index = jnp.arange(tile_rows, dtype=jnp.int32)
    same = (target_dev[:, None] == target_dev[None, :]) & (row_index[None, :] < row_index[:, None])
    slot_pos = jnp.sum(same.astype(jnp.int32), axis=1)
    slot = target_dev * capacity + slot_pos
    chosen = slot[:, None] == jnp.arange(slots, dtype=jnp.int32)[None, :]
    asked = jnp.sum(jnp.where(chosen, target_tile[:, None], 0), axis=0).reshape(
        group_size, capacity
    )
    wanted = lax.all_to_all(asked, "inner", split_axis=0, concat_axis=0, tiled=True).reshape(slots)
    piece = lax.all_gather(expander, "inner", axis=0, tiled=True)
    first_embed = jnp.dot(first_rows, piece, preferred_element_type=jnp.float32).astype(
        jnp.bfloat16
    )
    second_embed = jnp.dot(second_rows, piece, preferred_element_type=jnp.float32).astype(
        jnp.bfloat16
    )
    pick = (wanted[:, None] == row_index[None, :]).astype(jnp.bfloat16)
    send_rows = jnp.dot(pick, second_embed, preferred_element_type=jnp.float32).astype(jnp.bfloat16)
    recv_rows = lax.all_to_all(
        send_rows.reshape(group_size, capacity, expand_width),
        "inner",
        split_axis=0,
        concat_axis=0,
        tiled=True,
    ).reshape(slots, expand_width)
    partner = jnp.dot(chosen.astype(jnp.bfloat16), recv_rows, preferred_element_type=jnp.float32)
    counts = lax.dynamic_index_in_dim(tile_count, outer_pos, 0, keepdims=False)
    own_count = lax.dynamic_index_in_dim(counts, inner_pos, 0, keepdims=False)
    live = row_index < own_count
    dest_count = jnp.sum(
        jnp.where(
            target_dev[:, None] == jnp.arange(group_size, dtype=jnp.int32)[None, :],
            counts[None, :],
            0,
        ),
        axis=1,
    )
    valid = live & (target_tile < dest_count)
    diff = first_embed.astype(jnp.float32) - partner
    invariance = jnp.where(valid, jnp.mean(diff * diff, axis=-1), jnp.float32(0.0))
    masked = jnp.where(live[:, None], first_embed, jnp.zeros_like(first_embed))
    column_total = lax.psum(jnp.sum(masked.astype(jnp.float32), axis=0), ("inner", "outer"))
    total = jnp.sum(tile_count).astype(jnp.float32)
    share_rows = expand_width // group_size
    local_share = lax.psum_scatter(
        lax.dot_general(
            masked, masked, (((0,), (0,)), ((), ())), preferred_element_type=jnp.float32
        ),
        "inner",
        scatter_dimension=0,
        tiled=True,
    )
    gram_share = lax.psum(local_share, "outer")
    own_sums = lax.dynamic_slice_in_dim(column_total, inner_pos * share_rows, share_rows, 0)
    covariance = (gram_share - own_sums[:, None] * column_total[None, :] / total) / (total - 1.0)
    return (covariance, invariance[None, :])


def solution(mesh):
    return jax.shard_map(
        shards,
        mesh=mesh,
        in_specs=(
            P("outer", "inner", None),
            P("outer", "inner", None),
            P("inner", None),
            P(),
            P("outer", "inner", None),
            P("outer", "inner"),
        ),
        out_specs=(P("inner", None), P("outer", "inner")),
        check_vma=False,
    )
```

profile of v0, /device:TPU:0, one launch (start us, length us, event | category | flops | bytes accessed | tf_op | source)
XLA Modules:
  0.0 239.3 jit_solution(4994649485600865249)
XLA Ops:
  7.2 0.0 copy-start
  7.2 0.0 all-gather.2.cloned.1.call-start
  7.2 0.7 all-gather.2.cloned.1.call-update
  7.9 0.0 reduce-scatter.2.cloned.1.call-start
  8.0 1.3 dynamic_slice.11
  9.2 0.6 iota_compare_fusion.6
  9.9 79.7 %all-gather.2.cloned.1.call-done = bf16[2048,1024]{1,0:T(8,128)(2,1)} async-done(((bf16[128,1024]{1,0:T(8,128)(2,1)}), bf16[2048,1024]{1,0:T(8,128)(2,1)}) %all-gather.2.cloned.1.call-update) | async-done | bytes 4194320 | tf_op jit(solution)/shard_map/all_gather | solution.py:28
  89.6 3.8 %convert_reduce_fusion = (f32[1024]{0:T(1024)S(1)}, bf16[256,1024]{1,0:T(8,128)(2,1)S(1)}) fusion(pred[256]{0:T(512)(128)(4,1)S(1)} %iota_compare_fusion.6, bf16[2048,1024]{1,0:T(8,128)(2,1)} %all-gather.2.cloned.1.call-done, bf16[1,256,2048]{2,1,0:T(8,128)(2,1)} %param.6), kind=kOutput, calls=%fused_computation.8 | convolution fusion | flops 1074789376 | bytes 5771520 | tf_op jit(solution)/shard_map/dot_general | solution.py:29
  93.4 0.0 copy-start.1
  93.4 0.0 copy-start.2
  93.4 2.8 %fusion.8 = f32[1024,1024]{1,0:T(8,128)} fusion(bf16[256,1024]{1,0:T(8,128)(2,1)S(1)} %get-tuple-element.3, pred[256]{0:T(512)(128)(4,1)S(1)} %iota_compare_fusion.6), kind=kOutput, calls=%fused_computation.19 | convolution fusion | flops 537133056 | bytes 4718848 | tf_op jit(solution)/shard_map/dot_general | solution.py:64
  96.2 0.0 reduce-scatter.2.cloned.1.call-update
  96.2 0.0 copy-done.1
  96.2 0.2 convert_reduce_fusion.1
  96.4 0.0 copy-done.2
  96.4 0.2 select_reduce_fusion
  96.6 0.1 all_to_all.9
  96.7 11.4 %all_to_all.14 = s32[16,1,48]{2,1,0:T(1,128)S(1)} all-to-all(s32[16,1,48]{2,1,0:T(1,128)S(1)} %all_to_all.9), channel_id=1, replica_groups=mesh['inner'=16,'outer'=2] {'inner'}, dimensions={0} | all-to-all | bytes 6144 | tf_op jit(solution)/shard_map/all_to_all | solution.py:27
  108.0 0.5 broadcast.32
  108.5 0.7 reduce.3
  109.2 0.1 eq.66
  109.3 0.0 copy-done
  109.3 0.0 copy-start.3
  109.3 5.1 %convolution_convert_fusion = bf16[768,1024]{1,0:T(8,128)(2,1)} fusion(bf16[2048,1024]{1,0:T(8,128)(2,1)} %all-gather.2.cloned.1.call-done, bf16[1,256,2048]{2,1,0:T(8,128)(2,1)S(1)} %copy-done, s32[768]{0:T(1024)S(1)} %eq.66), kind=kOutput, calls=%fused_computation | convolution fusion | flops 1477640192 | bytes 6818816 | tf_op jit(solution)/shard_map/dot_general | solution.py:36
  114.4 3.8 %all-to-all-start.1 = ((bf16[16,48,1024]{2,1,0:T(8,128)(2,1)}), bf16[16,48,1024]{2,1,0:T(8,128)(2,1)S(1)}, u32[]{:S(2)}, u32[]{:S(2)}) async-start(bf16[16,48,1024]{2,1,0:T(8,128)(2,1)} %bitcast.22), calls=%async_computation.2 | async-start | bytes 3145728 | tf_op jit(solution)/shard_map/all_to_all | solution.py:37
  118.2 0.0 all-reduce.2.cloned.1.call-start
  118.3 0.0 copy-done.3
  118.3 0.6 reduce_sum.57
  119.6 0.1 select_reduce_fusion.1
  119.7 71.8 %psum.15 = f32[1024]{0:T(1024)S(1)} all-reduce(f32[1024]{0:T(1024)S(1)} %get-tuple-element.2), channel_id=1, replica_groups=mesh['inner'=16,'outer'=2] {'inner','outer'}, use_global_device_ids=true, to_apply=%region_3.4 | all-reduce | flops 1024 | bytes 8192 | tf_op jit(solution)/shard_map/psum | solution.py:60
  191.4 0.1 dynamic_slice.12
  191.5 0.0 all-to-all-done.1
  191.5 0.7 fusion.1
  192.3 19.4 %reduce-scatter.2.cloned.1.call-done = f32[64,1024]{1,0:T(8,128)} async-done(((f32[1024,1024]{1,0:T(8,128)}), f32[64,1024]{1,0:T(8,128)}) %reduce-scatter.2.cloned.1.call-update) | async-done | bytes 262160 | tf_op jit(solution)/shard_map/reduce_scatter | solution.py:63
  211.7 0.0 all-reduce.2.cloned.1.call-update
  211.7 1.2 and_select_fusion
  212.9 18.0 %all-reduce.2.cloned.1.call-done = f32[64,1024]{1,0:T(8,128)} async-done(((f32[64,1024]{1,0:T(8,128)}), f32[64,1024]{1,0:T(8,128)}) %all-reduce.2.cloned.1.call-update) | async-done | bytes 262160 | tf_op jit(solution)/shard_map/psum | solution.py:71
  231.0 1.8 subtract_divide_fusion
  (3 shorter events, 0.0 us)
Async XLA Ops:
  7.2 102.1 %copy-start = (bf16[1,256,2048]{2,1,0:T(8,128)(2,1)S(1)}, bf16[1,256,2048]{2,1,0:T(8,128)(2,1)}, u32[]{:S(2)}) copy-start(bf16[1,256,2048]{2,1,0:T(8,128)(2,1)} %param.7) | copy-start | bytes 3145732
  7.2 82.4 %all-gather.2.cloned.1.call-start = ((), (), s32[]{:S(2)}) async-start(), calls=%async_computation.3 | async-start | bytes 4456448 | tf_op jit(solution)/shard_map/all_gather | solution.py:28
  7.9 203.8 %reduce-scatter.2.cloned.1.call-start = ((), (), s32[]{:S(2)}) async-start(), calls=%async_computation.4 | async-start | bytes 4456448 | tf_op jit(solution)/shard_map/reduce_scatter | solution.py:63
  93.4 2.8 %copy-start.1 = (s32[1,256,1]{1,2,0:T(1,128)S(1)}, s32[1,256,1]{1,2,0:T(1,128)}, u32[]{:S(2)}) copy-start(s32[1,256,1]{1,2,0:T(1,128)} %param.10) | copy-start | bytes 3076
  93.4 3.0 %copy-start.2 = (s32[1,256]{1,0:T(1,128)S(1)}, s32[1,256]{1,0:T(1,128)}, u32[]{:S(2)}) copy-start(s32[1,256]{1,0:T(1,128)} %param.11) | copy-start | bytes 3076
  109.3 9.0 %copy-start.3 = (s32[2,16]{1,0:T(2,128)S(1)}, s32[2,16]{1,0:T(2,128)}, u32[]{:S(2)}) copy-start(s32[2,16]{1,0:T(2,128)} %param.9) | copy-start | bytes 388
  114.4 77.1 %all-to-all-start.1 = ((bf16[16,48,1024]{2,1,0:T(8,128)(2,1)}), bf16[16,48,1024]{2,1,0:T(8,128)(2,1)S(1)}, u32[]{:S(2)}, u32[]{:S(2)}) async-start(bf16[16,48,1024]{2,1,0:T(8,128)(2,1)} %bitcast.22), calls=%async_computation.2 | async-start | bytes 3145728 | tf_op jit(solution)/shard_map/all_to_all | solution.py:37
  118.2 112.8 %all-reduce.2.cloned.1.call-start = ((), (), s32[]{:S(2)}) async-start(), calls=%async_computation.5 | async-start | bytes 524288 | tf_op jit(solution)/shard_map/psum | solution.py:71
Sparse Core Ops, SparseCore 0:
  10.8 78.7 all-gather.1
  96.3 115.3 reduce-scatter.1
  214.0 16.9 all-reduce.1
where the time goes:
time: 240 us; the launch traced here: 239 us
  waiting for transfers between devices  118 us (49%)
  blocking collectives  83.1 us (35%)
  between operations  14.5 us (6%)
  matrix products  12.4 us (5%)
  other arithmetic  5.35 us (2%)
  starting transfers between devices  3.88 us (2%)
    all_gather x1, waiting for transfers between devices, shards(): piece = lax.all_gather(expander, 'inner', axis=0, tiled=True)  79.7 us
    psum x1, blocking collectives, shards(): lax.psum(jnp.sum(masked.astype(jnp.float32), axis=0), ('inner', 'outer'))  71.8 us
    reduce_scatter x1, waiting for transfers between devices, shards(): lax.psum_scatter(lax.dot_general(masked, masked, (((0,), (0,)), ((), ()))...  19.4 us
    psum x1, waiting for transfers between devices, shards(): gram_share = lax.psum(local_share, 'outer')  18 us
    all_to_all x1, blocking collectives, shards(): lax.all_to_all(asked, 'inner', split_axis=0, concat_axis=0, tiled=True)  11.4 us
    dot_general x1, matrix products, shards(): jnp.dot(pick, second_embed, preferred_element_type=jnp.float32)  5.14 us
  transfers between devices with their start and end apart: 4, of which 3 were waited for; matrix products, arithmetic and copies ran while one was open for 5% of the time, Pallas kernels for 0%

commit v1 on v0

--- a/solution.py
+++ b/solution.py
@@ -2,6 +2,37 @@
 import jax.numpy as jnp
 from jax import lax
 from jax.sharding import PartitionSpec as P
+
+
+def derive_the_blocks(local, which_dim, here_x):
+    formed, f_now = (local.shape[:which_dim], local.shape[which_dim + 1 :])
+    heard = local.reshape(*formed, here_x, -1, *f_now)
+    return jnp.moveaxis(heard, which_dim, 0)
+
+
+def cut_the_files(mine, where_dim):
+    mine = jnp.moveaxis(mine, 0, where_dim)
+    lower = mine.shape
+    return mine.reshape(
+        *lower[:where_dim], lower[where_dim] * lower[where_dim + 1], *lower[where_dim + 2 :]
+    )
+
+
+def bind_forms_up(payload, arr_in, a_name, slab_in):
+    after = lax.psum(1, a_name)
+    newest = lax.axis_index(a_name)
+    y_new, now = (after, newest)
+    u1 = derive_the_blocks(payload, arr_in, y_new)
+    z = u1
+    for nth in range(1, y_new):
+        z1, moved = ((now + nth) % y_new, (now - nth) % y_new)
+        response = lax.dynamic_index_in_dim(u1, z1, 0)
+        local_next = range(y_new)
+        state_now = map(lambda src_i: (src_i, (src_i + nth) % y_new), local_next)
+        low = list(state_now)
+        k_now = lax.ppermute(response, a_name, low)
+        z = lax.dynamic_update_slice_in_dim(z, k_now, moved, axis=0)
+    return cut_the_files(z, slab_in)
 
 
 def shards(feats_first, feats_second, expander, tile_count, match_dev, match_tile):
@@ -24,7 +55,7 @@
     asked = jnp.sum(jnp.where(chosen, target_tile[:, None], 0), axis=0).reshape(
         group_size, capacity
     )
-    wanted = lax.all_to_all(asked, "inner", split_axis=0, concat_axis=0, tiled=True).reshape(slots)
+    wanted = bind_forms_up(asked, 0, "inner", 0).reshape(slots)
     piece = lax.all_gather(expander, "inner", axis=0, tiled=True)
     first_embed = jnp.dot(first_rows, piece, preferred_element_type=jnp.float32).astype(
         jnp.bfloat16

time: 240 us -> 257 us (1.071)
  blocking collectives: 83.1 us -> 56 us
  waiting for transfers between devices: 118 us -> 142 us
  starting transfers between devices: 3.88 us -> 24.3 us
    ppermute x0 -> x15, waiting for transfers between devices: none -> 44.7 us  [bind_forms_up(): k_now = lax.ppermute(response, a_name, low)]
    reduce_scatter x1, waiting for transfers between devices: 19.4 us -> 0.02 us  [shards(): lax.psum_scatter(lax.dot_general(masked, masked, (((0,), (0,)), ((), ()))...]
    ppermute x0 -> x15, starting transfers between devices: none -> 17 us  [bind_forms_up(): k_now = lax.ppermute(response, a_name, low)]
    psum x1, blocking collectives: 71.8 us -> 56 us  [shards(): lax.psum(jnp.sum(masked.astype(jnp.float32), axis=0), ('inner', 'outer'))]
    all_to_all x1 -> x0, blocking collectives: 11.4 us -> none  [shards(): lax.all_to_all(asked, 'inner', split_axis=0, concat_axis=0, tiled=True)]
    all_to_all x1, starting transfers between devices: 3.76 us -> 7.14 us  [shards(): lax.all_to_all(send_rows.reshape(group_size, capacity, expand_width), 'in...]
  transfers between devices with their start and end apart: 4 -> 19, of which waited for: 3 -> 13; matrix products, arithmetic and copies ran while one was open for 5% -> 5% of each run, Pallas kernels for 0% -> 0%
where the time goes in v1:
time: 257 us
  waiting for transfers between devices  142 us (55%)
  blocking collectives  56 us (22%)
  starting transfers between devices  24.3 us (9%)
  between operations  14.6 us (6%)
  matrix products  12.4 us (5%)
  other arithmetic  5.35 us (2%)
    all_gather x1, waiting for transfers between devices, shards(): piece = lax.all_gather(expander, 'inner', axis=0, tiled=True)  79.7 us
    psum x1, blocking collectives, shards(): lax.psum(jnp.sum(masked.astype(jnp.float32), axis=0), ('inner', 'outer'))  56 us
    ppermute x15, waiting for transfers between devices, bind_forms_up(): k_now = lax.ppermute(response, a_name, low)  44.7 us
    ppermute x15, starting transfers between devices, bind_forms_up(): k_now = lax.ppermute(response, a_name, low)  17 us
    psum x1, waiting for transfers between devices, shards(): gram_share = lax.psum(local_share, 'outer')  16.9 us
    all_to_all x1, starting transfers between devices, shards(): lax.all_to_all(send_rows.reshape(group_size, capacity, expand_width), 'in...  7.14 us
  transfers between devices with their start and end apart: 19, of which 13 were waited for; matrix products, arithmetic and copies ran while one was open for 5% of the time, Pallas kernels for 0%

profile of v1, /device:TPU:0, one launch (start us, length us, event | category | flops | bytes accessed | tf_op | source)
XLA Modules:
  0.0 257.0 jit_solution(1716849974062889088)
XLA Ops:
  7.2 0.0 copy-start
  7.2 0.0 all-gather.2.cloned.1.call-start
  7.2 0.7 all-gather.2.cloned.1.call-update
  7.9 0.0 reduce-scatter.2.cloned.1.call-start
  8.0 1.3 dynamic_slice.57
  9.2 0.6 iota_compare_fusion.6
  9.9 79.7 %all-gather.2.cloned.1.call-done = bf16[2048,1024]{1,0:T(8,128)(2,1)} async-done(((bf16[128,1024]{1,0:T(8,128)(2,1)}), bf16[2048,1024]{1,0:T(8,128)(2,1)}) %all-gather.2.cloned.1.call-update) | async-done | bytes 4194320 | tf_op jit(solution)/shard_map/all_gather | solution.py:59
  89.6 3.8 %convert_reduce_fusion = (f32[1024]{0:T(1024)S(1)}, bf16[256,1024]{1,0:T(8,128)(2,1)S(1)}) fusion(pred[256]{0:T(512)(128)(4,1)S(1)} %iota_compare_fusion.6, bf16[2048,1024]{1,0:T(8,128)(2,1)} %all-gather.2.cloned.1.call-done, bf16[1,256,2048]{2,1,0:T(8,128)(2,1)} %param.6), kind=kOutput, calls=%fused_computation.8 | convolution fusion | flops 1074789376 | bytes 5771520 | tf_op jit(solution)/shard_map/dot_general | solution.py:60
  93.4 0.0 copy-start.1
  93.4 0.0 copy-start.2
  93.4 2.8 %fusion.8 = f32[1024,1024]{1,0:T(8,128)} fusion(bf16[256,1024]{1,0:T(8,128)(2,1)S(1)} %get-tuple-element.18, pred[256]{0:T(512)(128)(4,1)S(1)} %iota_compare_fusion.6), kind=kOutput, calls=%fused_computation.19 | convolution fusion | flops 537133056 | bytes 4718848 | tf_op jit(solution)/shard_map/dot_general | solution.py:95
  96.2 0.0 reduce-scatter.2.cloned.1.call-update
  96.2 0.0 copy-done.1
  96.2 0.2 convert_reduce_fusion.1
  96.4 0.2 select_reduce_fusion
  96.6 0.1 reshape_reshape.3
  96.7 1.5 collective-permute-start
  98.2 5.7 %collective-permute-done = s32[1,1,48]{2,1,0:T(1,128)S(1)} collective-permute-done((s32[1,1,48]{2,1,0:T(1,128)S(1)}, s32[1,1,48]{2,1,0:T(1,128)S(1)}, u32[]{:S(2)}, u32[]{:S(2)}) %collective-permute-start) | collective-permute-done | bytes 224 | tf_op jit(solution)/shard_map/ppermute | solution.py:33
  103.9 0.1 collective-permute-start.14
  104.0 0.6 collective-permute-start.13
  104.6 1.4 collective-permute-start.1
  106.1 1.5 collective-permute-start.12
  107.6 1.5 collective-permute-start.11
  109.1 1.8 collective-permute-done.1
  110.9 0.2 collective-permute-start.2
  111.0 6.1 %collective-permute-done.2 = s32[1,1,48]{2,1,0:T(1,128)S(1)} collective-permute-done((s32[1,1,48]{2,1,0:T(1,128)S(1)}, s32[1,1,48]{2,1,0:T(1,128)S(1)}, u32[]{:S(2)}, u32[]{:S(2)}) %collective-permute-start.2) | collective-permute-done | bytes 224 | tf_op jit(solution)/shard_map/ppermute | solution.py:33
  117.1 0.0 collective-permute-start.3
  117.1 5.3 %collective-permute-done.3 = s32[1,1,48]{2,1,0:T(1,128)S(1)} collective-permute-done((s32[1,1,48]{2,1,0:T(1,128)S(1)}, s32[1,1,48]{2,1,0:T(1,128)S(1)}, u32[]{:S(2)}, u32[]{:S(2)}) %collective-permute-start.3) | collective-permute-done | bytes 224 | tf_op jit(solution)/shard_map/ppermute | solution.py:33
  122.5 0.0 collective-permute-start.4
  122.5 6.3 %collective-permute-done.4 = s32[1,1,48]{2,1,0:T(1,128)S(1)} collective-permute-done((s32[1,1,48]{2,1,0:T(1,128)S(1)}, s32[1,1,48]{2,1,0:T(1,128)S(1)}, u32[]{:S(2)}, u32[]{:S(2)}) %collective-permute-start.4) | collective-permute-done | bytes 224 | tf_op jit(solution)/shard_map/ppermute | solution.py:33
  128.8 0.0 collective-permute-start.5
  128.8 5.4 %collective-permute-done.5 = s32[1,1,48]{2,1,0:T(1,128)S(1)} collective-permute-done((s32[1,1,48]{2,1,0:T(1,128)S(1)}, s32[1,1,48]{2,1,0:T(1,128)S(1)}, u32[]{:S(2)}, u32[]{:S(2)}) %collective-permute-start.5) | collective-permute-done | bytes 224 | tf_op jit(solution)/shard_map/ppermute | solution.py:33
  134.2 0.8 collective-permute-start.6
  135.0 4.5 %collective-permute-done.6 = s32[1,1,48]{2,1,0:T(1,128)S(1)} collective-permute-done((s32[1,1,48]{2,1,0:T(1,128)S(1)}, s32[1,1,48]{2,1,0:T(1,128)S(1)}, u32[]{:S(2)}, u32[]{:S(2)}) %collective-permute-start.6) | collective-permute-done | bytes 224 | tf_op jit(solution)/shard_map/ppermute | solution.py:33
  139.5 0.8 collective-permute-start.7
  140.3 3.7 %collective-permute-done.7 = s32[1,1,48]{2,1,0:T(1,128)S(1)} collective-permute-done((s32[1,1,48]{2,1,0:T(1,128)S(1)}, s32[1,1,48]{2,1,0:T(1,128)S(1)}, u32[]{:S(2)}, u32[]{:S(2)}) %collective-permute-start.7) | collective-permute-done | bytes 224 | tf_op jit(solution)/shard_map/ppermute | solution.py:33
  144.0 2.6 %collective-permute-start.8 = (s32[1,1,48]{2,1,0:T(1,128)S(1)}, s32[1,1,48]{2,1,0:T(1,128)S(1)}, u32[]{:S(2)}, u32[]{:S(2)}) collective-permute-start(s32[1,1,48]{2,1,0:T(1,128)S(1)} %get-tuple-element.8), channel_id=1, source_target_pairs={{0,18},{2,20},{4,22},{6,24},{8,26},{10,28},{12,30},{14,0},{16,2},{... | collective-permute-start | bytes 584 | tf_op jit(solution)/shard_map/ppermute | solution.py:33
  146.6 2.8 %collective-permute-done.8 = s32[1,1,48]{2,1,0:T(1,128)S(1)} collective-permute-done((s32[1,1,48]{2,1,0:T(1,128)S(1)}, s32[1,1,48]{2,1,0:T(1,128)S(1)}, u32[]{:S(2)}, u32[]{:S(2)}) %collective-permute-start.8) | collective-permute-done | bytes 224 | tf_op jit(solution)/shard_map/ppermute | solution.py:33
  149.3 2.6 %collective-permute-start.9 = (s32[1,1,48]{2,1,0:T(1,128)S(1)}, s32[1,1,48]{2,1,0:T(1,128)S(1)}, u32[]{:S(2)}, u32[]{:S(2)}) collective-permute-start(s32[1,1,48]{2,1,0:T(1,128)S(1)} %get-tuple-element.7), channel_id=1, source_target_pairs={{0,20},{2,22},{4,24},{6,26},{8,28},{10,30},{12,0},{14,2},{16,4},{1... | collective-permute-start | bytes 584 | tf_op jit(solution)/shard_map/ppermute | solution.py:33
  151.9 1.9 collective-permute-done.9
  153.8 3.5 %collective-permute-start.10 = (s32[1,1,48]{2,1,0:T(1,128)S(1)}, s32[1,1,48]{2,1,0:T(1,128)S(1)}, u32[]{:S(2)}, u32[]{:S(2)}) collective-permute-start(s32[1,1,48]{2,1,0:T(1,128)S(1)} %get-tuple-element.6), channel_id=1, source_target_pairs={{0,22},{2,24},{4,26},{6,28},{8,30},{10,0},{12,2},{14,4},{16,6},{18... | collective-permute-start | bytes 584 | tf_op jit(solution)/shard_map/ppermute | solution.py:33
  157.2 1.3 collective-permute-done.10
  158.5 0.0 collective-permute-done.11
  158.5 0.0 collective-permute-done.12
  158.6 0.0 collective-permute-done.13
  158.6 0.0 collective-permute-done.14
  158.6 0.5 broadcast.62
  159.1 0.7 reduce.3
  159.8 0.1 eq.97
  159.9 5.1 %convolution_convert_fusion = bf16[768,1024]{1,0:T(8,128)(2,1)} fusion(bf16[2048,1024]{1,0:T(8,128)(2,1)} %all-gather.2.cloned.1.call-done, bf16[1,256,2048]{2,1,0:T(8,128)(2,1)S(1)} %copy-done, s32[768]{0:T(1024)S(1)} %eq.97), kind=kOutput, calls=%fused_computation | convolution fusion | flops 1477640192 | bytes 6818816 | tf_op jit(solution)/shard_map/dot_general | solution.py:67
  165.0 7.1 %all-to-all-start = ((bf16[16,48,1024]{2,1,0:T(8,128)(2,1)}), bf16[16,48,1024]{2,1,0:T(8,128)(2,1)S(1)}, u32[]{:S(2)}, u32[]{:S(2)}) async-start(bf16[16,48,1024]{2,1,0:T(8,128)(2,1)} %bitcast.22), calls=%async_computation.1 | async-start | bytes 3145728 | tf_op jit(solution)/shard_map/all_to_all | solution.py:68
  172.2 0.0 all-reduce.2.cloned.1.call-start
  172.2 0.0 copy-done.3
  172.2 0.6 reduce_sum.57
  173.5 0.1 select_reduce_fusion.1
  173.6 56.0 %psum.15 = f32[1024]{0:T(1024)S(1)} all-reduce(f32[1024]{0:T(1024)S(1)} %get-tuple-element.17), channel_id=1, replica_groups=mesh['inner'=16,'outer'=2] {'inner','outer'}, use_global_device_ids=true, to_apply=%region_3.4 | all-reduce | flops 1024 | bytes 8192 | tf_op jit(solution)/shard_map/psum | solution.py:91
  229.7 0.1 dynamic_slice.58
  229.7 0.0 all-to-all-done
  229.7 0.7 fusion.1
  230.5 0.0 reduce-scatter.2.cloned.1.call-done
  230.5 0.0 all-reduce.2.cloned.1.call-update
  230.5 1.2 and_select_fusion
  231.8 16.9 %all-reduce.2.cloned.1.call-done = f32[64,1024]{1,0:T(8,128)} async-done(((f32[64,1024]{1,0:T(8,128)}), f32[64,1024]{1,0:T(8,128)}) %all-reduce.2.cloned.1.call-update) | async-done | bytes 262160 | tf_op jit(solution)/shard_map/psum | solution.py:102
  248.7 1.8 subtract_divide_fusion
  (22 shorter events, 0.2 us)
Async XLA Ops:
  7.2 152.7 %copy-start = (bf16[1,256,2048]{2,1,0:T(8,128)(2,1)S(1)}, bf16[1,256,2048]{2,1,0:T(8,128)(2,1)}, u32[]{:S(2)}) copy-start(bf16[1,256,2048]{2,1,0:T(8,128)(2,1)} %param.7) | copy-start | bytes 3145732
  7.2 82.4 %all-gather.2.cloned.1.call-start = ((), (), s32[]{:S(2)}) async-start(), calls=%async_computation.2 | async-start | bytes 4456448 | tf_op jit(solution)/shard_map/all_gather | solution.py:59
  7.9 222.6 %reduce-scatter.2.cloned.1.call-start = ((), (), s32[]{:S(2)}) async-start(), calls=%async_computation.3 | async-start | bytes 4456448 | tf_op jit(solution)/shard_map/reduce_scatter | solution.py:94
  93.4 2.9 %copy-start.1 = (s32[1,256,1]{1,2,0:T(1,128)S(1)}, s32[1,256,1]{1,2,0:T(1,128)}, u32[]{:S(2)}) copy-start(s32[1,256,1]{1,2,0:T(1,128)} %param.10) | copy-start | bytes 3076
  93.4 3.0 %copy-start.2 = (s32[1,256]{1,0:T(1,128)S(1)}, s32[1,256]{1,0:T(1,128)}, u32[]{:S(2)}) copy-start(s32[1,256]{1,0:T(1,128)} %param.11) | copy-start | bytes 3076
  96.7 7.2 %collective-permute-start = (s32[1,1,48]{2,1,0:T(1,128)S(1)}, s32[1,1,48]{2,1,0:T(1,128)S(1)}, u32[]{:S(2)}, u32[]{:S(2)}) collective-permute-start(s32[1,1,48]{2,1,0:T(1,128)S(1)} %constant_dynamic-slice_fusion.14), channel_id=1, source_target_pairs={{0,2},{2,4},{4,6},{6,8},{8,10},{10,12},{12,14},{14,16},{16,18},{18... | collective-permute-start | bytes 584 | tf_op jit(solution)/shard_map/ppermute | solution.py:33
  103.9 54.7 %collective-permute-start.14 = (s32[1,1,48]{2,1,0:T(1,128)S(1)}, s32[1,1,48]{2,1,0:T(1,128)S(1)}, u32[]{:S(2)}, u32[]{:S(2)}) collective-permute-start(s32[1,1,48]{2,1,0:T(1,128)S(1)} %get-tuple-element.2), channel_id=1, source_target_pairs={{0,30},{2,0},{4,2},{6,4},{8,6},{10,8},{12,10},{14,12},{16,14},{18,... | collective-permute-start | bytes 584 | tf_op jit(solution)/shard_map/ppermute | solution.py:33
  104.0 54.6 %collective-permute-start.13 = (s32[1,1,48]{2,1,0:T(1,128)S(1)}, s32[1,1,48]{2,1,0:T(1,128)S(1)}, u32[]{:S(2)}, u32[]{:S(2)}) collective-permute-start(s32[1,1,48]{2,1,0:T(1,128)S(1)} %get-tuple-element.3), channel_id=1, source_target_pairs={{0,28},{2,30},{4,0},{6,2},{8,4},{10,6},{12,8},{14,10},{16,12},{18,... | collective-permute-start | bytes 584 | tf_op jit(solution)/shard_map/ppermute | solution.py:33
  104.6 6.2 %collective-permute-start.1 = (s32[1,1,48]{2,1,0:T(1,128)S(1)}, s32[1,1,48]{2,1,0:T(1,128)S(1)}, u32[]{:S(2)}, u32[]{:S(2)}) collective-permute-start(s32[1,1,48]{2,1,0:T(1,128)S(1)} %get-tuple-element.15), channel_id=1, source_target_pairs={{0,4},{2,6},{4,8},{6,10},{8,12},{10,14},{12,16},{14,18},{16,20},{1... | collective-permute-start | bytes 584 | tf_op jit(solution)/shard_map/ppermute | solution.py:33
  106.1 52.5 %collective-permute-start.12 = (s32[1,1,48]{2,1,0:T(1,128)S(1)}, s32[1,1,48]{2,1,0:T(1,128)S(1)}, u32[]{:S(2)}, u32[]{:S(2)}) collective-permute-start(s32[1,1,48]{2,1,0:T(1,128)S(1)} %get-tuple-element.4), channel_id=1, source_target_pairs={{0,26},{2,28},{4,30},{6,0},{8,2},{10,4},{12,6},{14,8},{16,10},{18,... | collective-permute-start | bytes 584 | tf_op jit(solution)/shard_map/ppermute | solution.py:33
  107.6 51.0 %collective-permute-start.11 = (s32[1,1,48]{2,1,0:T(1,128)S(1)}, s32[1,1,48]{2,1,0:T(1,128)S(1)}, u32[]{:S(2)}, u32[]{:S(2)}) collective-permute-start(s32[1,1,48]{2,1,0:T(1,128)S(1)} %get-tuple-element.5), channel_id=1, source_target_pairs={{0,24},{2,26},{4,28},{6,30},{8,0},{10,2},{12,4},{14,6},{16,8},{18,... | collective-permute-start | bytes 584 | tf_op jit(solution)/shard_map/ppermute | solution.py:33
  110.9 6.2 %collective-permute-start.2 = (s32[1,1,48]{2,1,0:T(1,128)S(1)}, s32[1,1,48]{2,1,0:T(1,128)S(1)}, u32[]{:S(2)}, u32[]{:S(2)}) collective-permute-start(s32[1,1,48]{2,1,0:T(1,128)S(1)} %get-tuple-element.14), channel_id=1, source_target_pairs={{0,6},{2,8},{4,10},{6,12},{8,14},{10,16},{12,18},{14,20},{16,22},{... | collective-permute-start | bytes 584 | tf_op jit(solution)/shard_map/ppermute | solution.py:33
  117.1 5.3 %collective-permute-start.3 = (s32[1,1,48]{2,1,0:T(1,128)S(1)}, s32[1,1,48]{2,1,0:T(1,128)S(1)}, u32[]{:S(2)}, u32[]{:S(2)}) collective-permute-start(s32[1,1,48]{2,1,0:T(1,128)S(1)} %get-tuple-element.13), channel_id=1, source_target_pairs={{0,8},{2,10},{4,12},{6,14},{8,16},{10,18},{12,20},{14,22},{16,24},... | collective-permute-start | bytes 584 | tf_op jit(solution)/shard_map/ppermute | solution.py:33
  122.5 6.4 %collective-permute-start.4 = (s32[1,1,48]{2,1,0:T(1,128)S(1)}, s32[1,1,48]{2,1,0:T(1,128)S(1)}, u32[]{:S(2)}, u32[]{:S(2)}) collective-permute-start(s32[1,1,48]{2,1,0:T(1,128)S(1)} %get-tuple-element.12), channel_id=1, source_target_pairs={{0,10},{2,12},{4,14},{6,16},{8,18},{10,20},{12,22},{14,24},{16,26}... | collective-permute-start | bytes 584 | tf_op jit(solution)/shard_map/ppermute | solution.py:33
  128.8 5.4 %collective-permute-start.5 = (s32[1,1,48]{2,1,0:T(1,128)S(1)}, s32[1,1,48]{2,1,0:T(1,128)S(1)}, u32[]{:S(2)}, u32[]{:S(2)}) collective-permute-start(s32[1,1,48]{2,1,0:T(1,128)S(1)} %get-tuple-element.11), channel_id=1, source_target_pairs={{0,12},{2,14},{4,16},{6,18},{8,20},{10,22},{12,24},{14,26},{16,28}... | collective-permute-start | bytes 584 | tf_op jit(solution)/shard_map/ppermute | solution.py:33
  134.2 5.3 %collective-permute-start.6 = (s32[1,1,48]{2,1,0:T(1,128)S(1)}, s32[1,1,48]{2,1,0:T(1,128)S(1)}, u32[]{:S(2)}, u32[]{:S(2)}) collective-permute-start(s32[1,1,48]{2,1,0:T(1,128)S(1)} %get-tuple-element.10), channel_id=1, source_target_pairs={{0,14},{2,16},{4,18},{6,20},{8,22},{10,24},{12,26},{14,28},{16,30}... | collective-permute-start | bytes 584 | tf_op jit(solution)/shard_map/ppermute | solution.py:33
  139.5 4.4 %collective-permute-start.7 = (s32[1,1,48]{2,1,0:T(1,128)S(1)}, s32[1,1,48]{2,1,0:T(1,128)S(1)}, u32[]{:S(2)}, u32[]{:S(2)}) collective-permute-start(s32[1,1,48]{2,1,0:T(1,128)S(1)} %get-tuple-element.9), channel_id=1, source_target_pairs={{0,16},{2,18},{4,20},{6,22},{8,24},{10,26},{12,28},{14,30},{16,0},... | collective-permute-start | bytes 584 | tf_op jit(solution)/shard_map/ppermute | solution.py:33
  144.0 5.3 %collective-permute-start.8 = (s32[1,1,48]{2,1,0:T(1,128)S(1)}, s32[1,1,48]{2,1,0:T(1,128)S(1)}, u32[]{:S(2)}, u32[]{:S(2)}) collective-permute-start(s32[1,1,48]{2,1,0:T(1,128)S(1)} %get-tuple-element.8), channel_id=1, source_target_pairs={{0,18},{2,20},{4,22},{6,24},{8,26},{10,28},{12,30},{14,0},{16,2},{... | collective-permute-start | bytes 584 | tf_op jit(solution)/shard_map/ppermute | solution.py:33
  149.3 4.4 %collective-permute-start.9 = (s32[1,1,48]{2,1,0:T(1,128)S(1)}, s32[1,1,48]{2,1,0:T(1,128)S(1)}, u32[]{:S(2)}, u32[]{:S(2)}) collective-permute-start(s32[1,1,48]{2,1,0:T(1,128)S(1)} %get-tuple-element.7), channel_id=1, source_target_pairs={{0,20},{2,22},{4,24},{6,26},{8,28},{10,30},{12,0},{14,2},{16,4},{1... | collective-permute-start | bytes 584 | tf_op jit(solution)/shard_map/ppermute | solution.py:33
  153.8 4.8 %collective-permute-start.10 = (s32[1,1,48]{2,1,0:T(1,128)S(1)}, s32[1,1,48]{2,1,0:T(1,128)S(1)}, u32[]{:S(2)}, u32[]{:S(2)}) collective-permute-start(s32[1,1,48]{2,1,0:T(1,128)S(1)} %get-tuple-element.6), channel_id=1, source_target_pairs={{0,22},{2,24},{4,26},{6,28},{8,30},{10,0},{12,2},{14,4},{16,6},{18... | collective-permute-start | bytes 584 | tf_op jit(solution)/shard_map/ppermute | solution.py:33
  159.9 12.3 %copy-start.3 = (s32[2,16]{1,0:T(2,128)S(1)}, s32[2,16]{1,0:T(2,128)}, u32[]{:S(2)}) copy-start(s32[2,16]{1,0:T(2,128)} %param.9) | copy-start | bytes 388
  165.0 64.7 %all-to-all-start = ((bf16[16,48,1024]{2,1,0:T(8,128)(2,1)}), bf16[16,48,1024]{2,1,0:T(8,128)(2,1)S(1)}, u32[]{:S(2)}, u32[]{:S(2)}) async-start(bf16[16,48,1024]{2,1,0:T(8,128)(2,1)} %bitcast.22), calls=%async_computation.1 | async-start | bytes 3145728 | tf_op jit(solution)/shard_map/all_to_all | solution.py:68
  172.2 76.5 %all-reduce.2.cloned.1.call-start = ((), (), s32[]{:S(2)}) async-start(), calls=%async_computation.4 | async-start | bytes 524288 | tf_op jit(solution)/shard_map/psum | solution.py:102
Sparse Core Ops, SparseCore 0:
  10.8 78.7 all-gather.1
  96.3 112.4 reduce-scatter.1
  230.6 17.9 all-reduce.1
